TPU v7x, 128 devices: a whole 4x4x4 slice. The times are simulated.
128 devices in a mesh: section: 2 (over z_hi), render: 4 (over z_lo, core), dp: 16 (over y, x).
Axes of the slice: x: 4, y: 4, z: 4 (z_hi: 2, z_lo: 2; z = z_hi * 2 + z_lo), core: 2. Of those that a mesh axis runs over, the one named last changes fastest.
Arguments:
- section_tokens: bfloat16 [2, 16, 512, 2048], P('section', 'dp', 'render'), may hold values from -60 to 60
- w_qkv: bfloat16 [2, 2048, 3072], P('section', 'dp'), may hold values from -0.5 to 0.5
- w_out: bfloat16 [2, 1024, 2048], P('section', 'dp'), may hold values from -0.1875 to 0.1875
- gains: float32 [2, 2048], P('section'), may hold values from 0.25 to 1.75
- cotangent: bfloat16 [16, 512, 2048], P('dp', 'render'), may hold values from -6 to 6
Outputs:
- token_grads: bfloat16 [2, 16, 512, 2048], P('section', 'dp', 'render')
- qkv_grads: float32 [2, 2048, 3072], P('section', 'dp')
- out_grads: float32 [2, 1024, 2048], P('section', 'dp')
- gain_grads: float32 [2, 2048], P('section')
All inputs are finite; a program needn't handle non-finite values.
Results may differ from a plain program's by a relative error of at most 0.02.
Values may be sent and summed in bfloat16 or wider, within the bound.
No kernel may reach another device: no remote copies, remote signals or barrier semaphores. Data moves between devices by JAX's collectives and lax.ppermute only.
A program may use at most 192 MiB of HBM per device.

v0:
```python
import jax
import jax.numpy as jnp
from jax import lax
from jax.sharding import PartitionSpec as P

HEADS = 8
HD = 128


NORM_EPSILON = 1e-06


def joined_along(blocks, dim):
    blocks = jnp.moveaxis(blocks, 0, dim)
    lengths = blocks.shape
    return blocks.reshape(*lengths[:dim], lengths[dim] * lengths[dim + 1], *lengths[dim + 2 :])


def sent_to_all(shard, axis):
    peers = lax.axis_size(axis)
    return lax.all_to_all(
        jnp.broadcast_to(shard[None], (peers, *shard.shape)), axis, 0, 0, tiled=True
    )


def gather_directly(shard, axis, dim):
    return joined_along(sent_to_all(shard, axis), dim)


def shifted(block, axis, distance):
    devices = range(lax.axis_size(axis))
    route = [(i - distance, i) for i in devices if i - distance in devices]
    return lax.ppermute(block, axis, route)


def split_up(shard, dim, peers):
    lengths = shard.shape
    blocks = shard.reshape(*lengths[:dim], peers, lengths[dim] // peers, *lengths[dim + 1 :])
    return jnp.moveaxis(blocks, dim, 0)


def sum_at_owner(shard, axis, dim):
    blocks = split_up(shard, dim, lax.axis_size(axis))
    arrived = lax.all_to_all(blocks, axis, split_axis=0, concat_axis=0, tiled=True)
    return arrived.astype(jnp.float32).sum(axis=0)


def sent_together(arrays, axis, dim, along):
    widths = [a.shape[along] for a in arrays]
    both = jnp.concatenate(arrays, axis=along)
    out = lax.all_gather(both, axis, axis=dim, tiled=True)
    return tuple(jnp.split(out, [sum(widths[:k]) for k in range(1, len(widths))], axis=along))


def sum_packed(arrays, axis, dims):
    peers = lax.axis_size(axis)
    blocks = [split_up(a, dim, peers) for a, dim in zip(arrays, dims)]
    lines = jnp.concatenate([b.reshape(peers, -1) for b in blocks], axis=1)
    span = max(16, -(-lines.shape[1] // 1024) * 8)
    lines = jnp.pad(lines, ((0, 0), (0, span * 128 - lines.shape[1]))).reshape(-1, 128)
    line, at, finished = (lax.psum_scatter(lines, axis, tiled=True).reshape(-1), 0, [])
    for b in blocks:
        part = b[0]
        finished.append(line[at : at + part.size].reshape(part.shape))
        at += part.size
    return tuple(finished)


def gather_packed(arrays, axis, dims):
    line = jnp.concatenate([a.reshape(-1) for a in arrays])
    lines, at, finished = (lax.all_gather(line, axis), 0, [])
    for a, dim in zip(arrays, dims):
        blocks = lines[:, at : at + a.size].reshape(-1, *a.shape)
        finished.append(joined_along(blocks, dim))
        at += a.size
    return tuple(finished)


def over_copies(shard, axis):
    return sent_to_all(shard, axis).sum(axis=0)


def rms_norm(values, gain_row):
    wide_rows = values.astype(jnp.float32)
    row_scale = lax.rsqrt(jnp.mean(wide_rows * wide_rows, axis=-1, keepdims=True) + NORM_EPSILON)
    return ((wide_rows * row_scale * gain_row).astype(jnp.bfloat16), row_scale)


def norm_back(values, row_scale, gain_row, upstream):
    wide_rows = values.astype(jnp.float32)
    grad_wide = upstream.astype(jnp.float32)
    scaled = grad_wide * gain_row
    inner_sum = jnp.sum(scaled * wide_rows, axis=-1, keepdims=True)
    result = row_scale * scaled - wide_rows * row_scale**3 * inner_sum / values.shape[-1]
    gain_term = jnp.sum(grad_wide * wide_rows * row_scale, axis=0)
    return (result, gain_term)


def split_heads(values):
    return values.reshape(values.shape[0], HEADS, HD)


def only_when(flag, compute):

    def skipped():
        return jax.tree.map(jnp.zeros_like, compute())

    return lax.cond(flag, compute, skipped)


def attend(queries, key_rows, value_rows):
    factor = HD ** (-0.5)
    scores = (
        jnp.einsum(
            "qhd,khd->hqk",
            split_heads(queries),
            split_heads(key_rows),
            preferred_element_type=jnp.float32,
        )
        * factor
    )
    row_top = jnp.max(scores, axis=-1, keepdims=True)
    raised = jnp.exp(scores - row_top)
    row_total = jnp.sum(raised, axis=-1, keepdims=True)
    attn_prob = raised / row_total
    mixed_heads = jnp.einsum(
        "hqk,khd->qhd",
        attn_prob.astype(jnp.bfloat16),
        split_heads(value_rows),
        preferred_element_type=jnp.float32,
    )
    return (
        mixed_heads.reshape(queries.shape[0], HEADS * HD).astype(jnp.bfloat16),
        attn_prob,
        row_top,
        row_total,
    )


def score_grad(attn_prob, upstream, value_rows):
    factor = HD ** (-0.5)
    grad_prob = jnp.einsum(
        "qhd,khd->hqk",
        split_heads(upstream),
        split_heads(value_rows),
        preferred_element_type=jnp.float32,
    )
    row_delta = jnp.sum(grad_prob * attn_prob, axis=-1, keepdims=True)
    grad_score = (attn_prob * (grad_prob - row_delta) * factor).astype(jnp.bfloat16)
    return (grad_score, row_delta)


def key_terms_of(grad_score, attn_prob, queries, upstream):
    grad_key = jnp.einsum(
        "hqk,qhd->khd", grad_score, split_heads(queries), preferred_element_type=jnp.float32
    )
    grad_value = jnp.einsum(
        "hqk,qhd->khd",
        attn_prob.astype(jnp.bfloat16),
        split_heads(upstream),
        preferred_element_type=jnp.float32,
    )
    key_count = grad_key.shape[0]
    return (grad_key.reshape(key_count, HEADS * HD), grad_value.reshape(key_count, HEADS * HD))


def key_side(queries, upstream, row_top, row_total, row_delta, key_rows, value_rows):
    factor = HD ** (-0.5)
    scores = (
        jnp.einsum(
            "qhd,khd->hqk",
            split_heads(queries),
            split_heads(key_rows),
            preferred_element_type=jnp.float32,
        )
        * factor
    )
    attn_prob = jnp.exp(scores - row_top) / row_total
    grad_prob = jnp.einsum(
        "qhd,khd->hqk",
        split_heads(upstream),
        split_heads(value_rows),
        preferred_element_type=jnp.float32,
    )
    grad_score = (attn_prob * (grad_prob - row_delta) * factor).astype(jnp.bfloat16)
    grad_key, grad_value = key_terms_of(grad_score, attn_prob, queries, upstream)
    return jnp.concatenate([grad_key, grad_value], 1).astype(jnp.bfloat16)


def shards(section_tokens, w_qkv, w_out, gains, cotangent):
    tokens = section_tokens[0, 0]
    upstream = cotangent[0]
    gain_row = gains[0]
    head_width = HEADS * HD
    half_rows = tokens.shape[0] // 2
    section_index = lax.axis_index("section")
    is_encoder = section_index == 0
    is_decoder = jnp.logical_not(is_encoder)
    full_qkv, full_out = (
        lax.all_gather(w_qkv[0], "dp", axis=0, tiled=True),
        lax.all_gather(w_out[0], "dp", axis=0, tiled=True),
    )
    normed, row_scale = rms_norm(tokens, gain_row)
    projected = jnp.dot(normed, full_qkv, preferred_element_type=jnp.float32).astype(jnp.bfloat16)
    own_kv = projected[:, head_width:]
    enc_query = projected[half_rows:, :head_width]
    all_kv = gather_directly(own_kv, "render", 0)

    def encoder_forward():
        enc_mixed, enc_prob, enc_top, enc_total = attend(
            enc_query, all_kv[:, :head_width], all_kv[:, head_width:]
        )
        latent = (
            tokens[half_rows:].astype(jnp.float32)
            + jnp.dot(enc_mixed, full_out, preferred_element_type=jnp.float32)
        ).astype(jnp.bfloat16)
        return (enc_mixed, enc_prob, enc_top, enc_total, latent)

    enc_mixed, enc_prob, enc_top, enc_total, latent = only_when(is_encoder, encoder_forward)
    arrived = shifted(latent, "section", 1)

    def latent_project():
        lat_norm, lat_scale = rms_norm(arrived, gain_row)
        lat_kv = jnp.dot(
            lat_norm, full_qkv[:, head_width:], preferred_element_type=jnp.float32
        ).astype(jnp.bfloat16)
        return (lat_norm, lat_scale, lat_kv)

    lat_norm, lat_scale, lat_kv = only_when(is_decoder, latent_project)
    scene_kv = gather_directly(lat_kv, "render", 0)
    lat_count = scene_kv.shape[0]

    def decoder_attention():
        key_rows = jnp.concatenate(
            [scene_kv[:, :head_width], projected[:, head_width : 2 * head_width]], 0
        )
        value_rows = jnp.concatenate([scene_kv[:, head_width:], projected[:, 2 * head_width :]], 0)
        dec_query = projected[:, :head_width]
        dec_mixed, dec_prob, dec_top, dec_total = attend(dec_query, key_rows, value_rows)
        dec_out_part = jnp.einsum(
            "nc,nd->cd", dec_mixed, upstream, preferred_element_type=jnp.float32
        ).astype(jnp.bfloat16)
        grad_mixed = jnp.einsum(
            "nd,cd->nc", upstream, full_out, preferred_element_type=jnp.float32
        ).astype(jnp.bfloat16)
        dec_score, dec_delta = score_grad(dec_prob, grad_mixed, value_rows)
        dec_grad_query = jnp.einsum(
            "hqk,khd->qhd", dec_score, split_heads(key_rows), preferred_element_type=jnp.float32
        ).reshape(dec_query.shape[0], head_width)
        dec_grad_key, dec_grad_value = key_terms_of(dec_score, dec_prob, dec_query, grad_mixed)
        lat_terms = jnp.concatenate([dec_grad_key[:lat_count], dec_grad_value[:lat_count]], 1)
        dec_grad_proj = jnp.concatenate(
            [dec_grad_query, dec_grad_key[lat_count:], dec_grad_value[lat_count:]], 1
        ).astype(jnp.bfloat16)
        return (lat_terms, dec_grad_proj, dec_out_part)

    lat_terms, dec_grad_proj, dec_out_part = only_when(is_decoder, decoder_attention)
    lat_grad = sum_at_owner(lat_terms.astype(jnp.bfloat16), "render", 0).astype(jnp.bfloat16)

    def decoder_finish():
        dec_qkv_part = jnp.einsum(
            "nd,nc->dc", normed, dec_grad_proj, preferred_element_type=jnp.float32
        )
        lat_weight_part = jnp.einsum(
            "nd,nc->dc", lat_norm, lat_grad, preferred_element_type=jnp.float32
        )
        dec_qkv_part = dec_qkv_part.at[:, head_width:].add(lat_weight_part).astype(jnp.bfloat16)
        grad_normed = jnp.einsum(
            "nc,dc->nd", dec_grad_proj, full_qkv, preferred_element_type=jnp.float32
        ).astype(jnp.bfloat16)
        grad_lat_norm = jnp.einsum(
            "nc,dc->nd", lat_grad, full_qkv[:, head_width:], preferred_element_type=jnp.float32
        ).astype(jnp.bfloat16)
        dec_back, dec_gain_first = norm_back(tokens, row_scale, gain_row, grad_normed)
        dec_result = (upstream.astype(jnp.float32) + dec_back).astype(jnp.bfloat16)
        lat_back, dec_gain_second = norm_back(arrived, lat_scale, gain_row, grad_lat_norm)
        return (
            dec_qkv_part,
            dec_result,
            lat_back.astype(jnp.bfloat16),
            dec_gain_first + dec_gain_second,
        )

    dec_qkv_part, dec_result, lat_back, dec_gain = only_when(is_decoder, decoder_finish)
    returned = shifted(lat_back, "section", -1)

    def encoder_back_queries():
        enc_values = all_kv[:, head_width:]
        enc_keys = all_kv[:, :head_width]
        enc_out_part = jnp.einsum(
            "nc,nd->cd", enc_mixed, returned, preferred_element_type=jnp.float32
        ).astype(jnp.bfloat16)
        grad_enc_mixed = jnp.einsum(
            "nd,cd->nc", returned, full_out, preferred_element_type=jnp.float32
        ).astype(jnp.bfloat16)
        enc_score, enc_delta = score_grad(enc_prob, grad_enc_mixed, enc_values)
        query_grad = (
            jnp.einsum(
                "hqk,khd->qhd", enc_score, split_heads(enc_keys), preferred_element_type=jnp.float32
            )
            .reshape(half_rows, head_width)
            .astype(jnp.bfloat16)
        )
        return (enc_out_part, grad_enc_mixed, enc_delta, query_grad)

    enc_out_part, grad_enc_mixed, enc_delta, query_grad = only_when(
        is_encoder, encoder_back_queries
    )
    all_query, all_upstream = sent_together((enc_query, grad_enc_mixed), "render", 0, 1)
    all_top, all_total, all_delta = sent_together((enc_top, enc_total, enc_delta), "render", 1, 0)

    def own_key_grads():
        return key_side(
            all_query,
            all_upstream,
            all_top,
            all_total,
            all_delta,
            own_kv[:, :head_width],
            own_kv[:, head_width:],
        )

    key_grad = only_when(is_encoder, own_key_grads)

    def encoder_finish():
        query_weight_part = jnp.einsum(
            "nd,nc->dc", normed[half_rows:], query_grad, preferred_element_type=jnp.float32
        )
        key_weight_part = jnp.einsum(
            "nd,nc->dc", normed, key_grad, preferred_element_type=jnp.float32
        )
        enc_qkv_part = jnp.concatenate([query_weight_part, key_weight_part], 1).astype(jnp.bfloat16)
        grad_enc_norm = jnp.einsum(
            "nc,dc->nd", key_grad, full_qkv[:, head_width:], preferred_element_type=jnp.float32
        )
        query_back = jnp.einsum(
            "nc,dc->nd", query_grad, full_qkv[:, :head_width], preferred_element_type=jnp.float32
        )
        grad_enc_norm = grad_enc_norm.at[half_rows:].add(query_back).astype(jnp.bfloat16)
        enc_back, enc_gain_term = norm_back(tokens, row_scale, gain_row, grad_enc_norm)
        enc_result = enc_back.at[half_rows:].add(returned.astype(jnp.float32)).astype(jnp.bfloat16)
        return (enc_qkv_part, enc_result, enc_gain_term)

    enc_qkv_part, enc_result, enc_gain_term = only_when(is_encoder, encoder_finish)
    token_grad = jnp.where(is_encoder, enc_result, dec_result)
    qkv_part = jnp.where(is_encoder, enc_qkv_part, dec_qkv_part).astype(jnp.float32)
    out_part = jnp.where(is_encoder, enc_out_part, dec_out_part).astype(jnp.float32)
    gain_part = jnp.where(is_encoder, enc_gain_term, dec_gain)
    qkv_total, out_total = (
        lax.psum_scatter(
            qkv_part.astype(jnp.bfloat16), "render", scatter_dimension=1, tiled=True
        ).astype(jnp.float32),
        lax.psum_scatter(
            out_part.astype(jnp.bfloat16), "render", scatter_dimension=1, tiled=True
        ).astype(jnp.float32),
    )
    qkv_total, out_total = tuple(
        (
            part.astype(jnp.float32)
            for part in sum_packed(
                (qkv_total.astype(jnp.bfloat16), out_total.astype(jnp.bfloat16)), "dp", (0, 0)
            )
        )
    )
    qkv_total, out_total = tuple(
        (
            part.astype(jnp.float32)
            for part in gather_packed(
                (qkv_total.astype(jnp.bfloat16), out_total.astype(jnp.bfloat16)), "render", (1, 1)
            )
        )
    )
    gain_total = over_copies(gain_part, ("render", "dp"))
    return (token_grad[None, None], qkv_total[None], out_total[None], gain_total[None])


def solution(mesh):
    in_specs = (
        P("section", "dp", "render", None),
        P("section", "dp", None),
        P("section", "dp", None),
        P("section", None),
        P("dp", "render", None),
    )
    out_specs = (
        P("section", "dp", "render", None),
        P("section", "dp", None),
        P("section", "dp", None),
        P("section", None),
    )
    return jax.shard_map(shards, mesh=mesh, in_specs=in_specs, out_specs=out_specs, check_vma=False)
```

profile of v0, /device:TPU:1, one launch (start us, length us, event | category | flops | bytes accessed | tf_op | source)
XLA Modules:
  0.0 694.2 jit_solution(12119105009085443958)
XLA Ops:
  9.9 1.2 fusion.123
  11.1 92.1 %all-gather.10.cloned.1.call-done = bf16[1,2048,3072]{2,1,0:T(8,128)(2,1)} async-done(((bf16[1,128,3072]{2,1,0:T(8,128)(2,1)}), bf16[1,2048,3072]{2,1,0:T(8,128)(2,1)}) %all-gather.10.cloned.1.call-update) | async-done | bytes 12582928 | tf_op jit(solution)/shard_map/all_gather | solution.py:200
  103.3 6.4 convolution_convert_fusion.11
  110.0 1.6 broadcast_in_dim.22
  111.6 5.1 all-to-all-start
  117.4 24.3 %all-to-all-done = bf16[4,128,2048]{1,2,0:T(8,128)(2,1)} async-done(((bf16[4,128,2048]{1,2,0:T(8,128)(2,1)}), bf16[4,128,2048]{1,2,0:T(8,128)(2,1)}, u32[]{:S(2)}, u32[]{:S(2)}) %all-to-all-start) | async-done | bytes 2097184 | tf_op jit(solution)/shard_map/all_to_all | solution.py:21
  141.6 2.9 copy.319
  144.6 12.0 %all-gather.12.cloned.1.call-done = bf16[1,1024,2048]{2,1,0:T(8,128)(2,1)} async-done(((bf16[1,64,2048]{2,1,0:T(8,128)(2,1)}), bf16[1,1024,2048]{2,1,0:T(8,128)(2,1)}) %all-gather.12.cloned.1.call-update) | async-done | bytes 4194320 | tf_op jit(solution)/shard_map/all_gather | solution.py:201
  156.5 13.9 %conditional.7 = (bf16[64,1024]{1,0:T(8,128)(2,1)}, f32[8,64,512]{2,1,0:T(8,128)}, f32[8,64,1]{1,0,2:T(8,128)}, f32[8,64,1]{1,0,2:T(8,128)}, bf16[64,2048]{1,0:T(8,128)(2,1)S(1)}) conditional(s32[]{:T(128)} %convert_element_type.206, () %tuple.79, (bf16[64,1024]{1,0:T(8,128)(2,1)}, bf16[512,2048]{1,0:T(8,128)(2,1)S(1)}, ...), branch_computations={%region_1.0_spmd, %region_2.0_spmd} | conditional | flops 404945920 | bytes 37890116 | solution.py:108
  156.5 2.5 copy.320
  159.1 1.7 fusion.126
  160.7 1.9 fusion.127
  162.6 1.8 fusion.3
  164.4 2.0 fusion.2
  166.3 1.7 fusion.1
  168.7 1.8 fusion
  171.2 1.3 collective-permute-start
  172.5 5.6 collective-permute-done
  179.9 5.4 all-to-all-start.1
  185.4 13.7 %all-to-all-done.1 = bf16[4,64,2048]{2,1,0:T(8,128)(2,1)} async-done(((bf16[4,64,2048]{2,1,0:T(8,128)(2,1)}), bf16[4,64,2048]{2,1,0:T(8,128)(2,1)}, u32[]{:S(2)}, u32[]{:S(2)}) %all-to-all-start.1) | async-done | bytes 1048608 | tf_op jit(solution)/shard_map/all_to_all | solution.py:21
  199.1 5.0 conditional.9
  201.1 2.5 broadcast.186
  204.1 2.3 copy.321
  206.4 5.1 all-to-all-start.2
  211.5 13.7 %all-to-all-done.2 = bf16[4,64,2048]{2,1,0:T(8,128)(2,1)} async-done(((bf16[4,64,2048]{2,1,0:T(8,128)(2,1)}), bf16[4,64,2048]{2,1,0:T(8,128)(2,1)}, u32[]{:S(2)}, u32[]{:S(2)}) %all-to-all-start.2) | async-done | bytes 1048608 | tf_op jit(solution)/shard_map/all_to_all | solution.py:44
  225.2 7.8 %conditional.10 = (bf16[128,2048]{1,0:T(8,128)(2,1)}, bf16[64,2048]{1,0:T(8,128)(2,1)}, f32[2048]{0:T(1024)S(1)}, bf16[2048,3072]{0,1:T(8,128)(2,1)}) conditional(s32[]{:T(128)} %convert_element_type.210, () %tuple.81, (bf16[128,2048]{1,0:T(8,128)(2,1)S(1)}, bf16[128,3072]{0,1:T(8,128)(2,1)}, bf16[4,64,2048]{2,1,0:T(8,128)(2,1)}, ...), branch_computations={%region_13.0_spmd, %region_14.20_spmd} | conditional | flops 4313053184 | bytes 156054880 | solution.py:108
  226.8 6.1 broadcast.189.clone
  233.0 1.3 collective-permute-start.1
  234.3 124.3 %collective-permute-done.1 = bf16[64,2048]{1,0:T(8,128)(2,1)S(1)} collective-permute-done((bf16[64,2048]{1,0:T(8,128)(2,1)}, bf16[64,2048]{1,0:T(8,128)(2,1)S(1)}, u32[]{:S(2)}, u32[]{:S(2)}) %collective-permute-start.1) | collective-permute-done | bytes 262176 | tf_op jit(solution)/shard_map/ppermute | solution.py:33
  358.7 15.2 %conditional.11 = (bf16[1024,2048]{1,0:T(8,128)(2,1)}, bf16[64,1024]{1,0:T(8,128)(2,1)S(1)}, f32[8,64,1]{1,0,2:T(8,128)}, bf16[64,1024]{1,0:T(8,128)(2,1)S(1)}) conditional(s32[]{:T(128)} %convert_element_type.206, () %tuple.78, (bf16[64,1024]{1,0:T(8,128)(2,1)}, bf16[64,2048]{1,0:T(8,128)(2,1)S(1)}, bf16[1024,2048]{1,0:T(8,128)(2,1)}, ...), branch_computations={%region_20.21_spmd, %region_21.23_spmd} | conditional | flops 674889216 | bytes 42209396 | solution.py:108
  358.9 2.5 copy.323
  361.4 1.8 fusion.131
  364.2 1.4 convolution_convert_fusion.6
  365.6 2.3 multiply_reduce_fusion.1
  367.9 1.7 fusion.82
  369.7 4.2 convolution_convert_fusion.5
  373.8 1.6 pad_maximum_fusion.7
  375.5 4.7 broadcast_select_fusion.1
  381.1 7.2 %all_gather.21 = f32[24,256,1]{0,2,1:T(1,128)S(1)} all-gather(f32[24,64,1]{0,2,1:T(1,128)S(1)} %copy.324), channel_id=1, replica_groups=mesh['section'=2,'render'=4,'dp'=16] {'render'}, dimensions={1}, use_global_device_ids=true | all-gather | bytes 30720 | tf_op jit(solution)/shard_map/all_gather | solution.py:51
  388.3 6.6 all-gather.8.cloned.1.call-done
  394.9 8.9 %conditional.12 = (bf16[128,2048]{0,1:T(8,128)(2,1)S(1)}) conditional(s32[]{:T(128)} %convert_element_type.206, () %tuple.88, (bf16[256,2048]{1,0:T(8,128)(2,1)}, bf16[128,2048]{1,0:T(8,128)(2,1)S(1)}, f32[24,256,1]{0,2,1:T(1,128)S(1)}) %tuple.191), branch_computations={%region_23.24_spmd, %region_24.0_spmd} | conditional | flops 271843328 | bytes 13754376 | solution.py:108
  396.7 1.5 copy.325
  398.3 1.9 fusion.93
  400.2 2.3 fusion.96
  403.8 32.5 %conditional.13 = (bf16[2048,3072]{0,1:T(8,128)(2,1)}, bf16[128,2048]{1,0:T(8,128)(2,1)}, f32[2048]{0:T(1024)S(1)}) conditional(s32[]{:T(128)} %convert_element_type.206, () %tuple.77, (bf16[128,2048]{1,0:T(8,128)(2,1)S(1)}, bf16[64,1024]{1,0:T(8,128)(2,1)S(1)}, bf16[128,2048]{0,1:T(8,128)(2,1)S(1)}, f32[128,1]{0,1:T(1,128)}, ...), branch_computations={%region_25.0_spmd, %region_26.29_spmd} | conditional | flops 2721184000 | bytes 65828460 | solution.py:108
  405.5 7.2 %fusion.101 = f32[128,2048]{1,0:T(8,128)S(1)} fusion(bf16[128,2048]{0,1:T(8,128)(2,1)} %copy-done.8, bf16[2048,3072]{1,0:T(8,128)(2,1)} %get-tuple-element.182), kind=kOutput, calls=%fused_computation.122 | convolution fusion | flops 1073741824 | bytes 9961472 | tf_op jit(solution)/shard_map/cond/branch_1_fun/nc,dc->nd/dot_general | solution.py:333
  412.7 3.6 fusion.108
  418.0 1.3 convolution_convert_fusion.10
  419.4 2.3 convolution_convert_fusion.9
  421.7 14.6 %pad_maximum_fusion.5 = bf16[2048,3072]{0,1:T(8,128)(2,1)} fusion(bf16[2048,2048]{0,1:T(8,128)(2,1)S(1)} %convolution_convert_fusion.9, bf16[2048,1024]{0,1:T(8,128)(2,1)S(1)} %convolution_convert_fusion.10), kind=kLoop, calls=%fused_computation.121 | loop fusion | flops 25165824 | bytes 25165824 | tf_op jit(solution)/shard_map/cond/branch_1_fun/concatenate | solution.py:332
  436.3 10.7 %broadcast_select_fusion = bf16[2048,3072]{0,1:T(8,128)(2,1)} fusion(bf16[2048,3072]{0,1:T(8,128)(2,1)} %get-tuple-element.228, bf16[2048,3072]{0,1:T(8,128)(2,1)} %get-tuple-element.472, pred[]{:T(512)S(6)} %eq.3), kind=kLoop, calls=%fused_computation.146 | loop fusion | flops 6291456 | bytes 37748736 | tf_op jit(solution)/shard_map/jit(_where)/select_n | solution.py:346
  447.3 2.3 reshape_reshape.7
  449.7 110.1 %reduce-scatter.4.cloned.1.call-done = bf16[2048,768]{0,1:T(8,128)(2,1)} async-done(((bf16[2048,3072]{0,1:T(8,128)(2,1)}), bf16[2048,768]{0,1:T(8,128)(2,1)}) %reduce-scatter.4.cloned.1.call-update) | async-done | bytes 3145744 | tf_op jit(solution)/shard_map/reduce_scatter | solution.py:350
  559.8 3.2 copy.330
  563.0 2.6 reshape_reshape.6
  565.6 4.4 pad_maximum_fusion.6
  570.0 4.9 reshape.278
  574.9 76.6 %reduce-scatter.8.cloned.1.call-done = bf16[1024,128]{1,0:T(8,128)(2,1)} async-done(((bf16[16384,128]{1,0:T(8,128)(2,1)}), bf16[1024,128]{1,0:T(8,128)(2,1)}) %reduce-scatter.8.cloned.1.call-update) | async-done | bytes 262160 | tf_op jit(solution)/shard_map/reduce_scatter | solution.py:61
  655.2 8.7 %all-to-all-start.3 = ((f32[64,1,2048]{2,1,0:T(1,128)}), f32[64,1,2048]{2,1,0:T(1,128)S(1)}, u32[]{:S(2)}, u32[]{:S(2)}) async-start(f32[64,1,2048]{2,1,0:T(1,128)} %broadcast_in_dim.29), calls=%async_computation.6 | async-start | bytes 1048576 | tf_op jit(solution)/shard_map/all_to_all | solution.py:21
  663.9 1.9 select_bitcast_fusion
  665.8 10.2 %all-to-all-done.3 = f32[64,1,2048]{2,1,0:T(1,128)S(1)} async-done(((f32[64,1,2048]{2,1,0:T(1,128)}), f32[64,1,2048]{2,1,0:T(1,128)S(1)}, u32[]{:S(2)}, u32[]{:S(2)}) %all-to-all-start.3) | async-done | bytes 524320 | tf_op jit(solution)/shard_map/all_to_all | solution.py:21
  677.0 4.5 all-gather.14.cloned.1.call-done
  681.5 1.6 reshape.287
  684.9 2.0 reshape.281
  (89 shorter events, 26.2 us)
Async XLA Ops:
  7.2 96.1 %all-gather.10.cloned.1.call-start = ((), (), s32[]{:S(2)}) async-start(), calls=%async_computation.11 | async-start | bytes 13369344 | tf_op jit(solution)/shard_map/all_gather | solution.py:200
  7.9 148.6 %all-gather.12.cloned.1.call-start = ((), (), s32[]{:S(2)}) async-start(), calls=%async_computation.12 | async-start | bytes 4456448 | tf_op jit(solution)/shard_map/all_gather | solution.py:201
  9.9 215.3 %copy-start.19 = (f32[128,1]{0,1:T(1,128)}, f32[128,1]{0,1:T(1,128)S(1)}, u32[]{:S(2)}) copy-start(f32[128,1]{0,1:T(1,128)S(1)} %get-tuple-element.506) | copy-start | bytes 1540
  109.6 7.1 %copy-start.3 = (bf16[128,3072]{1,0:T(8,128)(2,1)}, bf16[128,3072]{1,0:T(8,128)(2,1)S(1)}, u32[]{:S(2)}) copy-start(bf16[128,3072]{1,0:T(8,128)(2,1)S(1)} %convolution_convert_fusion.11) | copy-start | bytes 2359300
  109.7 1.9 copy-start.6
  111.6 30.0 %all-to-all-start = ((bf16[4,128,2048]{1,2,0:T(8,128)(2,1)}), bf16[4,128,2048]{1,2,0:T(8,128)(2,1)}, u32[]{:S(2)}, u32[]{:S(2)}) async-start(bf16[4,128,2048]{1,2,0:T(8,128)(2,1)} %broadcast_in_dim.22), calls=%async_computation | async-start | bytes 4194304 | tf_op jit(solution)/shard_map/all_to_all | solution.py:21
  116.7 39.8 %copy-start.2 = (bf16[1,1,128,2048]{3,2,1,0:T(8,128)(2,1)S(1)}, bf16[1,1,128,2048]{3,2,1,0:T(8,128)(2,1)}, u32[]{:S(2)}) copy-start(bf16[1,1,128,2048]{3,2,1,0:T(8,128)(2,1)} %param.25) | copy-start | bytes 1572868
  156.5 21.5 %copy-start.14 = (f32[1,2048]{1,0:T(1,128)S(1)}, f32[1,2048]{1,0:T(1,128)}, u32[]{:S(2)}) copy-start(f32[1,2048]{1,0:T(1,128)} %param.28) | copy-start | bytes 24580
  162.6 6.1 copy-start
  170.5 0.7 copy-start.15
  171.2 6.9 collective-permute-start
  179.9 19.1 %all-to-all-start.1 = ((bf16[4,64,2048]{2,1,0:T(8,128)(2,1)}), bf16[4,64,2048]{2,1,0:T(8,128)(2,1)}, u32[]{:S(2)}, u32[]{:S(2)}) async-start(bf16[4,64,2048]{2,1,0:T(8,128)(2,1)} %broadcast_in_dim.25), calls=%async_computation.1 | async-start | bytes 2097152 | tf_op jit(solution)/shard_map/all_to_all | solution.py:21
  206.4 18.8 %all-to-all-start.2 = ((bf16[4,64,2048]{2,1,0:T(8,128)(2,1)}), bf16[4,64,2048]{2,1,0:T(8,128)(2,1)}, u32[]{:S(2)}, u32[]{:S(2)}) async-start(bf16[4,64,2048]{2,1,0:T(8,128)(2,1)} %bitcast.193), calls=%async_computation.2 | async-start | bytes 2097152 | tf_op jit(solution)/shard_map/all_to_all | solution.py:44
  211.5 183.4 %all-gather.8.cloned.1.call-start = ((), (), s32[]{:S(2)}) async-start(), calls=%async_computation.7 | async-start | bytes 1310720 | tf_op jit(solution)/shard_map/all_gather | solution.py:51
  233.0 125.6 %copy-start.17 = (f32[2048]{0:T(1024)}, f32[2048]{0:T(1024)S(1)}, u32[]{:S(2)}) copy-start(f32[2048]{0:T(1024)S(1)} %get-tuple-element.233) | copy-start | bytes 24580
  233.0 125.6 %collective-permute-start.1 = (bf16[64,2048]{1,0:T(8,128)(2,1)}, bf16[64,2048]{1,0:T(8,128)(2,1)S(1)}, u32[]{:S(2)}, u32[]{:S(2)}) collective-permute-start(bf16[64,2048]{1,0:T(8,128)(2,1)} %get-tuple-element.219), channel_id=1, source_target_pairs={{64,0},{65,1},{66,2},{67,3},{68,4},{69,5},{70,6},{71,7},{72,8},{73... | collective-permute-start | bytes 786440 | tf_op jit(solution)/shard_map/ppermute | solution.py:33
  361.4 2.8 copy-start.1
  365.6 4.0 copy-start.11
  369.6 4.2 copy-start.12
  375.5 71.9 %reduce-scatter.6.cloned.1.call-start = ((), (), s32[]{:S(2)}) async-start(), calls=%async_computation.9 | async-start | bytes 5242880 | tf_op jit(solution)/shard_map/reduce_scatter | solution.py:353
  380.2 14.7 %copy-start.7 = (bf16[128,2048]{1,0:T(8,128)(2,1)S(1)}, bf16[128,2048]{1,0:T(8,128)(2,1)}, u32[]{:S(2)}) copy-start(bf16[128,2048]{1,0:T(8,128)(2,1)} %copy-done.6) | copy-start | bytes 1572868
  380.2 179.5 %reduce-scatter.4.cloned.1.call-start = ((), (), s32[]{:S(2)}) async-start(), calls=%async_computation.8 | async-start | bytes 15728640 | tf_op jit(solution)/shard_map/reduce_scatter | solution.py:350
  404.1 0.8 copy-start.8
  412.7 3.6 copy-start.20
  418.0 1.3 copy-start.9
  447.0 204.6 %reduce-scatter.8.cloned.1.call-start = ((), (), s32[]{:S(2)}) async-start(), calls=%async_computation.10 | async-start | bytes 4456448 | tf_op jit(solution)/shard_map/reduce_scatter | solution.py:61
  574.9 79.2 %copy-start.18 = (f32[2048]{0:T(1024)S(1)}, f32[2048]{0:T(1024)}, u32[]{:S(2)}) copy-start(f32[2048]{0:T(1024)} %copy-done.17) | copy-start | bytes 24580
  574.9 106.6 %all-gather.14.cloned.1.call-start = ((), (), s32[]{:S(2)}) async-start(), calls=%async_computation.13 | async-start | bytes 1310720 | tf_op jit(solution)/shard_map/all_gather | solution.py:71
  655.2 20.8 %all-to-all-start.3 = ((f32[64,1,2048]{2,1,0:T(1,128)}), f32[64,1,2048]{2,1,0:T(1,128)S(1)}, u32[]{:S(2)}, u32[]{:S(2)}) async-start(f32[64,1,2048]{2,1,0:T(1,128)} %broadcast_in_dim.29), calls=%async_computation.6 | async-start | bytes 1048576 | tf_op jit(solution)/shard_map/all_to_all | solution.py:21
Sparse Core Ops, SparseCore 0:
  10.1 93.0 all-gather.9
  105.4 51.1 all-gather.11
  375.6 19.2 all-gather.7
  397.2 46.0 reduce-scatter.5
  447.1 112.6 reduce-scatter.3
  575.0 76.4 reduce-scatter.7
  654.2 27.2 all-gather.13
where the time goes:
time: 702 us; the launch traced here: 694 us
  waiting for transfers between devices  495 us (71%)
  local copies, waits for them, and re-layouts  58 us (8%)
  other arithmetic  50.1 us (7%)
  matrix products  40.3 us (6%)
  starting transfers between devices  27.4 us (4%)
  between operations  14.8 us (2%)
  blocking collectives  7.17 us (1%)
    ppermute x2, waiting for transfers between devices, shifted(): return lax.ppermute(block, axis, route)  130 us
    reduce_scatter x1, waiting for transfers between devices, shards(): lax.psum_scatter(qkv_part.astype(jnp.bfloat16), 'render', scatter_dimensi...  110 us
    all_gather x1, waiting for transfers between devices, shards(): lax.all_gather(w_qkv[0], 'dp', axis=0, tiled=True)  92.1 us
    reduce_scatter x1, waiting for transfers between devices, sum_packed(): lax.psum_scatter(lines, axis, tiled=True).reshape(-1)  76.6 us
    all_to_all x3, waiting for transfers between devices, sent_to_all(): lax.all_to_all(jnp.broadcast_to(shard[None], (peers, *shard.shape)), axis...  48.2 us
    another operation x15, local copies, waits for them, and re-layouts  19.8 us
    all_to_all x3, starting transfers between devices, sent_to_all(): lax.all_to_all(jnp.broadcast_to(shard[None], (peers, *shard.shape)), axis...  19.2 us
    concatenate x1, other arithmetic, encoder_finish(): jnp.concatenate([query_weight_part, key_weight_part], 1)  14.6 us
  transfers between devices with their start and end apart: 13, of which 12 were waited for; matrix products, arithmetic and copies ran while one was open for 11% of the time, Pallas kernels for 0%

commit v1 on v0

v1 whole, which is shorter than its diff:
```python
import jax
import jax.numpy as jnp
from jax import lax
from jax.sharding import Mesh
from jax.sharding import PartitionSpec as P

HD = 128
MY = 2
MW = MY * HD
NORM_EPSILON = 1e-06
RENDER = ("zl", "core")
DP = ("y", "x")
SWAP = [(0, 1), (1, 0)]
DIAG = [(0, 3), (1, 2), (2, 1), (3, 0)]
bf16 = jnp.bfloat16
f32 = jnp.float32


def mm(left, right):
    return jnp.dot(left, right, preferred_element_type=f32)


def mm_tn(left, right):
    return lax.dot_general(left, right, (((0,), (0,)), ((), ())), preferred_element_type=f32)


def mm_nt(left, right):
    return lax.dot_general(left, right, (((1,), (1,)), ((), ())), preferred_element_type=f32)


def core_swap(t):
    return lax.ppermute(t, "core", SWAP)


def z_swap(t):
    return lax.ppermute(t, "zl", SWAP)


def gather_rel(t):
    z = z_swap(t)
    c = core_swap(t)
    return [t, c, z, core_swap(z)]


def spread_rel(b):
    return [b[0], core_swap(b[1]), z_swap(b[2]), lax.ppermute(b[3], RENDER, DIAG)]


def sum_rel(b0, b1, b2, b3):
    near, far = core_swap(b1), core_swap(b3)
    far = (b2.astype(f32) + far.astype(f32)).astype(bf16)
    return b0.astype(f32) + near.astype(f32) + z_swap(far).astype(f32)


def rows_of(j, t):
    n = t.shape[0] // 4
    return [t[(i ^ j) * n : ((i ^ j) + 1) * n] for i in range(4)]


def sum_dp(t):
    blocks = t.reshape(16, t.shape[0] // 16, t.shape[1])
    return lax.all_to_all(blocks, DP, 0, 0, tiled=True).astype(f32).sum(axis=0)


def rms_norm(values, gain_row):
    wide = values.astype(f32)
    scale = lax.rsqrt(jnp.mean(wide * wide, axis=-1, keepdims=True) + NORM_EPSILON)
    return (wide * scale * gain_row).astype(bf16), scale


def norm_back(values, scale, gain_row, upstream):
    wide = values.astype(f32)
    grad = upstream.astype(f32)
    scaled = grad * gain_row
    inner = jnp.sum(scaled * wide, axis=-1, keepdims=True)
    result = scale * scaled - wide * scale**3 * inner / values.shape[-1]
    return result, jnp.sum(grad * wide * scale, axis=0)


def heads(t):
    return [t[:, h * HD : (h + 1) * HD] for h in range(MY)]


FACTOR = HD**-0.5


def softmax(scores):
    top = jnp.max(scores, axis=-1, keepdims=True)
    raised = jnp.exp(scores - top)
    return raised / jnp.sum(raised, axis=-1, keepdims=True)


def encoder_forward(q, k, v):
    probs, outs = [], []
    for qh, kh, vh in zip(heads(q), heads(k), heads(v)):
        p = softmax(mm_nt(qh, kh) * FACTOR)
        probs.append(p)
        outs.append(mm(p.astype(bf16), vh).astype(bf16))
    return jnp.concatenate(outs, 1), jnp.stack(probs)


def encoder_backward(q, k, v, probs, up):
    dq, dk, dv = [], [], []
    for h, (qh, kh, vh, uh) in enumerate(zip(heads(q), heads(k), heads(v), heads(up))):
        p = probs[h]
        dp = mm_nt(uh, vh)
        delta = jnp.sum(dp * p, axis=-1, keepdims=True)
        ds = (p * (dp - delta) * FACTOR).astype(bf16)
        dq.append(mm(ds, kh).astype(bf16))
        dk.append(mm_tn(ds, qh).astype(bf16))
        dv.append(mm_tn(p.astype(bf16), uh).astype(bf16))
    return jnp.concatenate(dq, 1), jnp.concatenate(dk + dv, 1)


def decoder_attention(q, k, v, kz, vz, up):
    out, dq, dk, dv, dkz, dvz = [], [], [], [], [], []
    views = q.shape[0] // 128
    lat = kz.shape[0]

    def per_view(a, b):
        return lax.dot_general(
            a.reshape(views, 128, -1), b.reshape(views, 128, -1),
            (((2,), (2,)), ((0,), (0,))), preferred_element_type=f32,
        ).reshape(views * 128, 128)

    def own_mm(p, b):
        return lax.dot_general(
            p.reshape(views, 128, 128), b.reshape(views, 128, HD),
            (((2,), (1,)), ((0,), (0,))), preferred_element_type=f32,
        ).reshape(views * 128, HD)

    def own_tn(p, b):
        return lax.dot_general(
            p.reshape(views, 128, 128), b.reshape(views, 128, HD),
            (((1,), (1,)), ((0,), (0,))), preferred_element_type=f32,
        ).reshape(views * 128, HD)

    for qh, kh, vh, kzh, vzh, uh in zip(*map(heads, (q, k, v, kz, vz, up))):
        s = jnp.concatenate([mm_nt(qh, kzh), per_view(qh, kh)], 1) * FACTOR
        p = softmax(s)
        pb = p.astype(bf16)
        out.append((mm(pb[:, :lat], vzh) + own_mm(pb[:, lat:], vh)).astype(bf16))
        dp = jnp.concatenate([mm_nt(uh, vzh), per_view(uh, vh)], 1)
        delta = jnp.sum(dp * p, axis=-1, keepdims=True)
        ds = (p * (dp - delta) * FACTOR).astype(bf16)
        dq.append((mm(ds[:, :lat], kzh) + own_mm(ds[:, lat:], kh)).astype(bf16))
        dk.append(own_tn(ds[:, lat:], qh).astype(bf16))
        dv.append(own_tn(pb[:, lat:], uh).astype(bf16))
        dkz.append(mm_tn(ds[:, :lat], qh).astype(bf16))
        dvz.append(mm_tn(pb[:, :lat], uh).astype(bf16))
    cat = jnp.concatenate
    return cat(out, 1), cat(dq + dk + dv, 1), cat(dkz + dvz, 1)


def shards(section_tokens, w_qkv, w_out, gains, cotangent):
    tokens = section_tokens[0, 0]
    upstream = cotangent[0]
    gain_row = gains[0]
    width = tokens.shape[1]
    rank = lax.axis_index("zl") * 2 + lax.axis_index("core")
    is_encoder = lax.axis_index("section") == 0
    half = tokens.shape[0] // 2

    mine = w_qkv[0].reshape(-1, 3, 4, MW)
    mine = lax.dynamic_index_in_dim(mine, rank, 2, keepdims=False).reshape(-1, 3 * MW)
    w_h = lax.all_gather(mine, DP, axis=0, tiled=True)
    cols = width // 4
    out_mine = lax.dynamic_slice_in_dim(w_out[0], rank * cols, cols, 1)
    w_col = lax.all_gather(out_mine, DP, axis=0, tiled=True).reshape(4, MW, cols)
    w_rel = [lax.dynamic_index_in_dim(w_col, rank ^ j, 0, keepdims=False) for j in range(4)]
    order = [rank ^ j for j in range(4)]

    def absolute(blocks, dim):
        both = jnp.stack(blocks)
        return jnp.concatenate(
            [lax.dynamic_index_in_dim(both, i, 0, keepdims=False) for i in order], dim
        )

    rows = jnp.concatenate(gather_rel(tokens), 0)
    ups = jnp.concatenate(gather_rel(upstream), 0)
    normed, scales = rms_norm(rows, gain_row)
    scale = scales[: tokens.shape[0]]
    projected = mm(normed, w_h).astype(bf16)
    q, k, v = projected[:, :MW], projected[:, MW : 2 * MW], projected[:, 2 * MW :]
    w_row = absolute(spread_rel(w_rel), 1)

    def latents(t):
        return t.reshape(4, 2 * half, -1)[:, half:].reshape(4 * half, -1)

    lat_q = latents(q)
    enc_o, enc_p = lax.cond(
        is_encoder,
        lambda: encoder_forward(lat_q, k, v),
        lambda: (jnp.zeros((4 * half, MW), bf16), jnp.zeros((MY, 4 * half, k.shape[0]), f32)),
    )
    enc_all = [jnp.concatenate(rows_of(j, t), 0) for j, t in enumerate(gather_rel(enc_o))]
    lat_cols = lax.dynamic_slice_in_dim(latents(rows), rank * cols, cols, 1).astype(f32)
    z_cols = (
        lat_cols + mm(jnp.concatenate(enc_all, 1), jnp.concatenate(w_rel, 0))
    ).astype(bf16)
    z_cols = lax.ppermute(z_cols, "section", [(0, 1)])
    z_blocks = [jnp.concatenate(rows_of(j, t), 0) for j, t in enumerate(gather_rel(z_cols))]
    z = absolute(z_blocks, 1)
    up_o = mm_nt(ups, w_row).astype(bf16)

    def decoder():
        nz, z_scales = rms_norm(z, gain_row)
        kvz = mm(nz, w_h[:, MW:]).astype(bf16)
        o, d_proj, d_kvz = decoder_attention(q, k, v, kvz[:, :MW], kvz[:, MW:], up_o)
        d_nz = mm_nt(d_kvz, w_h[:, MW:]).astype(bf16)
        return o, d_proj, d_kvz, nz, z_scales[:half], d_nz

    dec_o, d_proj, d_kvz, nz, z_scale, d_nz = lax.cond(
        jnp.logical_not(is_encoder),
        decoder,
        lambda: (
            jnp.zeros((rows.shape[0], MW), bf16),
            jnp.zeros((rows.shape[0], 3 * MW), bf16),
            jnp.zeros((4 * half, 2 * MW), bf16),
            jnp.zeros((4 * half, width), bf16),
            jnp.zeros((half, 1), f32),
            jnp.zeros((4 * half, width), bf16),
        ),
    )
    d_nz = sum_rel(*[d_nz[j * half : (j + 1) * half] for j in range(4)]).astype(bf16)
    d_z, z_gain = norm_back(z[:half], z_scale, gain_row, d_nz)
    z_gain = jnp.where(is_encoder, 0.0, z_gain)
    d_z = lax.ppermute(d_z.astype(bf16), "section", [(1, 0)])
    d_z_all = jnp.concatenate(gather_rel(d_z), 0)

    dec_all = [jnp.concatenate(rows_of(j, t), 0) for j, t in enumerate(gather_rel(dec_o))]

    def encoder_back():
        up_e = mm_nt(d_z_all, w_row).astype(bf16)
        dq, dkv = encoder_backward(lat_q, k, v, enc_p, up_e)
        dq = jnp.pad(dq.reshape(4, half, MW), ((0, 0), (half, 0), (0, 0))).reshape(-1, MW)
        proj = jnp.concatenate([dq, dkv], 1)
        return proj, mm_tn(normed, proj).astype(bf16)

    def decoder_back():
        part = mm_tn(normed, d_proj)
        part = part.at[:, MW:].add(mm_tn(nz, d_kvz))
        return d_proj, part.astype(bf16)

    d_proj, qkv_part = lax.cond(is_encoder, encoder_back, decoder_back)

    def my_cols(t):
        return lax.dynamic_slice_in_dim(t, rank * cols, cols, 1)

    out_part = lax.cond(
        is_encoder,
        lambda: mm_tn(absolute(enc_all, 1), my_cols(d_z_all)).astype(bf16),
        lambda: mm_tn(absolute(dec_all, 1), my_cols(ups)).astype(bf16),
    )
    out_sum = sum_dp(out_part).astype(bf16)
    qkv_sum = sum_dp(qkv_part).astype(bf16)
    out_total = absolute(gather_rel(out_sum), 1).astype(f32)
    qkv_blocks = jnp.stack(gather_rel(qkv_sum)).reshape(4, -1, 3, MW)
    qkv_total = jnp.stack(
        [lax.dynamic_index_in_dim(qkv_blocks, i, 0, keepdims=False) for i in order], 2
    )
    qkv_total = qkv_total.reshape(-1, 12 * MW).astype(f32)

    d_n = mm_nt(d_proj, w_h).astype(bf16)
    n = tokens.shape[0]
    d_n = sum_rel(*[d_n[j * n : (j + 1) * n] for j in range(4)]).astype(bf16)
    back, gain_part = norm_back(tokens, scale, gain_row, d_n)
    residual = jnp.where(
        is_encoder,
        jnp.pad(d_z.astype(f32), ((half, 0), (0, 0))),
        upstream.astype(f32),
    )
    token_grad = (back + residual).astype(bf16)
    gain_total = lax.psum(gain_part + z_gain, RENDER + DP)
    return token_grad[None, None], qkv_total[None], out_total[None], gain_total[None]


def solution(mesh):
    fine = Mesh(mesh.devices.reshape(2, 2, 2, 4, 4), ("section", "zl", "core", "y", "x"))
    in_specs = (
        P("section", DP, RENDER, None),
        P("section", DP, None),
        P("section", DP, None),
        P("section", None),
        P(DP, RENDER, None),
    )
    out_specs = (
        P("section", DP, RENDER, None),
        P("section", DP, None),
        P("section", DP, None),
        P("section", None),
    )
    return jax.shard_map(shards, mesh=fine, in_specs=in_specs, out_specs=out_specs, check_vma=False)
```

time: 702 us -> 519 us (0.74)
  waiting for transfers between devices: 495 us -> 191 us
  blocking collectives: 7.17 us -> 140 us
  starting transfers between devices: 27.4 us -> 60.8 us
  other arithmetic: 50.1 us -> 28 us
  local copies, waits for them, and re-layouts: 58 us -> 40.7 us
  matrix products: 40.3 us -> 32.3 us
    reduce_scatter x3 -> x0, waiting for transfers between devices: 187 us -> none  [the longest x1 110 us: shards(): lax.psum_scatter(qkv_part.astype(jnp.bfloat16), 'render', scatter_dimensi...]
    psum x0 -> x1, blocking collectives: none -> 140 us  [shards(): gain_total = lax.psum(gain_part + z_gain, RENDER + DP)]
    all_gather x4 -> x2, waiting for transfers between devices: 115 us -> 50.7 us  [the longest x1 26 us: shards(): lax.all_gather(out_mine, DP, axis=0, tiled=True).reshape(4, MW, cols)]
    all_to_all x4 -> x2, waiting for transfers between devices: 61.9 us -> 0.01 us  [sum_dp(): return lax.all_to_all(blocks, DP, 0, 0, tiled=True).astype(f32).sum(axis=0)]
    ppermute x2 -> x35, starting transfers between devices: 2.59 us -> 49.3 us  [the longest x21 33.8 us: core_swap(): return lax.ppermute(t, 'core', SWAP)]
    another operation x17 -> x9, local copies, waits for them, and re-layouts: 24.8 us -> 4.69 us
    select_n x3 -> x0, other arithmetic: 15.4 us -> none  [the longest x1 10.7 us: shards(): jnp.where(is_encoder, enc_qkv_part, dec_qkv_part).astype(jnp.float32)]
    concatenate x6 -> x10, other arithmetic: 23.1 us -> 8.43 us  [the longest x1 3.07 us: shards(): ups = jnp.concatenate(gather_rel(upstream), 0)]
  transfers between devices with their start and end apart: 13 -> 39, of which waited for: 12 -> 17; matrix products, arithmetic and copies ran while one was open for 11% -> 16% of each run, Pallas kernels for 0% -> 0%
where the time goes in v1:
time: 519 us; the launch traced here: 509 us
  waiting for transfers between devices  191 us (37%)
  blocking collectives  140 us (27%)
  starting transfers between devices  60.8 us (12%)
  local copies, waits for them, and re-layouts  40.7 us (8%)
  matrix products  32.3 us (6%)
  other arithmetic  28 us (5%)
  between operations  15.2 us (3%)
    psum x1, blocking collectives, shards(): gain_total = lax.psum(gain_part + z_gain, RENDER + DP)  140 us
    ppermute x1, waiting for transfers between devices, shards(): d_z = lax.ppermute(d_z.astype(bf16), 'section', [(1, 0)])  78.7 us
    ppermute x11, waiting for transfers between devices, z_swap(): return lax.ppermute(t, 'zl', SWAP)  48.6 us
    ppermute x21, starting transfers between devices, core_swap(): return lax.ppermute(t, 'core', SWAP)  33.8 us
    all_gather x1, waiting for transfers between devices, shards(): lax.all_gather(out_mine, DP, axis=0, tiled=True).reshape(4, MW, cols)  26 us
    all_gather x1, waiting for transfers between devices, shards(): w_h = lax.all_gather(mine, DP, axis=0, tiled=True)  24.7 us
    dot_general x7, matrix products, mm_nt(): lax.dot_general(left, right, (((1,), (1,)), ((), ())), preferred_element_...  13.5 us
    all_to_all x2, starting transfers between devices, sum_dp(): return lax.all_to_all(blocks, DP, 0, 0, tiled=True).astype(f32).sum(axis=0)  11.3 us
  transfers between devices with their start and end apart: 39, of which 17 were waited for; matrix products, arithmetic and copies ran while one was open for 16% of the time, Pallas kernels for 0%

profile of v1, /device:TPU:1, one launch (start us, length us, event | category | flops | bytes accessed | tf_op | source)
XLA Modules:
  0.0 508.7 jit_solution(4999467450770316148)
XLA Ops:
  7.2 1.6 copy.191
  9.6 2.5 collective-permute-start.1
  13.2 10.6 %collective-permute-done.1 = bf16[128,2048]{1,0:T(8,128)(2,1)S(1)} collective-permute-done((bf16[128,2048]{1,0:T(8,128)(2,1)S(1)}, bf16[128,2048]{1,0:T(8,128)(2,1)S(1)}, u32[]{:S(2)}, u32[]{:S(2)}) %collective-permute-start.1) | collective-permute-done | bytes 524320 | tf_op jit(solution)/shard_map/ppermute | solution.py:36
  23.8 2.1 collective-permute-start.2
  26.6 8.5 %collective-permute-done.11 = bf16[128,2048]{1,0:T(8,128)(2,1)} collective-permute-done((bf16[128,2048]{1,0:T(8,128)(2,1)}, bf16[128,2048]{1,0:T(8,128)(2,1)}, u32[]{:S(2)}, u32[]{:S(2)}) %collective-permute-start.11) | collective-permute-done | bytes 524320 | tf_op jit(solution)/shard_map/ppermute | solution.py:36
  35.1 1.3 collective-permute-start.12
  37.2 1.6 fusion.127
  38.8 1.9 fusion.129
  40.8 24.7 %all-gather.4.cloned.1.call-done = bf16[2048,768]{0,1:T(8,128)(2,1)} async-done(((bf16[128,768]{0,1:T(8,128)(2,1)}), bf16[2048,768]{0,1:T(8,128)(2,1)}) %all-gather.4.cloned.1.call-update) | async-done | bytes 3145744 | tf_op jit(solution)/shard_map/all_gather | solution.py:166
  65.5 4.4 convolution_convert_fusion.20
  71.4 5.6 %conditional.8 = (bf16[256,256]{0,1:T(8,128)(2,1)S(1)}, f32[2,256,512]{2,1,0:T(8,128)S(1)}) conditional(s32[]{:T(128)} %convert_element_type.262, () %tuple.46, (bf16[256,256]{1,0:T(8,128)(2,1)}, bf16[512,256]{1,0:T(8,128)(2,1)S(1)}, bf16[512,256]{1,0:T(8,128)(2,1)}) %tuple.47), branch_computations={%region_1.2_spmd, %region_2.7_spmd} | conditional | flops 137165824 | bytes 8402960 | solution.py:191
  77.8 1.3 collective-permute-start.4
  79.0 3.1 pad_maximum_fusion.10
  83.2 26.0 %all-gather.6.cloned.1.call-done = bf16[1,1024,512]{2,1,0:T(8,128)(2,1)} async-done(((bf16[1,64,512]{2,1,0:T(8,128)(2,1)}), bf16[1,1024,512]{2,1,0:T(8,128)(2,1)}) %all-gather.6.cloned.1.call-update) | async-done | bytes 1048592 | tf_op jit(solution)/shard_map/all_gather | solution.py:169
  109.1 1.3 constant_dynamic-slice_fusion.8
  110.4 2.2 collective-permute-start.13
  112.6 1.3 collective-permute-start.14
  116.1 1.4 fusion.131
  117.6 4.8 collective-permute-start.6
  122.4 4.3 collective-permute-done.15
  127.0 3.8 collective-permute-done.6
  130.9 1.5 convolution_convert_fusion.21
  134.4 3.3 collective-permute-done.8
  137.7 1.8 collective-permute-start.9
  141.8 4.7 conditional.9
  148.2 1.5 pad_maximum_fusion.22
  151.4 1.4 collective-permute-start.18
  152.7 4.9 collective-permute-done.30
  157.7 1.6 collective-permute-start.31
  159.3 3.9 collective-permute-done.18
  163.2 1.3 fusion.154
  164.8 1.3 collective-permute-start.19
  166.1 78.7 %collective-permute-done.19 = bf16[64,2048]{1,0:T(8,128)(2,1)S(1)} collective-permute-done((bf16[64,2048]{1,0:T(8,128)(2,1)S(1)}, bf16[64,2048]{1,0:T(8,128)(2,1)S(1)}, u32[]{:S(2)}, u32[]{:S(2)}) %collective-permute-start.19) | collective-permute-done | bytes 262176 | tf_op jit(solution)/shard_map/ppermute | solution.py:228
  244.8 1.5 collective-permute-start.20
  246.6 7.7 %collective-permute-done.21 = bf16[64,2048]{1,0:T(8,128)(2,1)S(1)} collective-permute-done((bf16[64,2048]{1,0:T(8,128)(2,1)S(1)}, bf16[64,2048]{1,0:T(8,128)(2,1)S(1)}, u32[]{:S(2)}, u32[]{:S(2)}) %collective-permute-start.21) | collective-permute-done | bytes 262176 | tf_op jit(solution)/shard_map/ppermute | solution.py:36
  257.2 3.7 conditional.11
  259.4 1.5 fusion.116
  261.9 4.7 all-to-all-start.1
  266.7 2.3 pad_maximum_fusion.14
  269.0 27.9 %conditional.10 = (bf16[512,768]{1,0:T(8,128)(2,1)}, bf16[2048,768]{1,0:T(8,128)(2,1)S(1)}) conditional(s32[]{:T(128)} %convert_element_type.262, (bf16[512,2048]{1,0:T(8,128)(2,1)S(1)}, bf16[512,768]{0,1:T(8,128)(2,1)}, bf16[256,2048]{1,0:T(8,128)(2,1)}, bf16[256,512]{0,1:T(8,128)(2,1)}) %tuple.169, (f32[2,256,512]{2,1,0:T(8,128)S(1)}, ...), branch_computations={%region_17.18_spmd, %region_18.21_spmd} | conditional | flops 2151284224 | bytes 29884432 | solution.py:245
  269.0 2.0 convolution_convert_fusion.16
  272.2 1.3 fusion.90
  275.1 1.7 copy.186
  278.4 1.8 convolution_convert_fusion.15
  280.2 1.7 copy.187
  281.9 1.6 constant_dynamic-update-slice_fusion.7
  283.5 1.7 convolution_convert_fusion.14
  289.0 4.7 fusion.84
  293.7 3.2 copy.227
  296.9 2.8 copy.199
  299.7 5.3 %convolution_convert_fusion.19 = bf16[512,2048]{1,0:T(8,128)(2,1)} fusion(bf16[512,768]{1,0:T(8,128)(2,1)} %get-tuple-element.155, bf16[2048,768]{0,1:T(8,128)(2,1)} %all-gather.4.cloned.1.call-done), kind=kOutput, calls=%fused_computation.208 | convolution fusion | flops 1611661312 | bytes 6029312 | tf_op jit(solution)/shard_map/dot_general | solution.py:28
  305.0 6.6 %all-to-all-start = ((bf16[16,128,768]{1,2,0:T(8,128)(2,1)}), bf16[16,128,768]{1,2,0:T(8,128)(2,1)S(1)}, u32[]{:S(2)}, u32[]{:S(2)}) async-start(bf16[16,128,768]{1,2,0:T(8,128)(2,1)} %copy.199), calls=%async_computation | async-start | bytes 6291456 | tf_op jit(solution)/shard_map/all_to_all | solution.py:62
  311.6 2.1 fusion.186
  314.9 2.3 collective-permute-done.24
  317.2 2.0 add_convert_fusion.1
  319.6 1.4 reduce_sum.154
  321.0 1.3 collective-permute-start.33
  324.6 9.6 %collective-permute-done.33 = bf16[64,512]{1,0:T(8,128)(2,1)S(1)} collective-permute-done((bf16[64,512]{1,0:T(8,128)(2,1)S(1)}, bf16[64,512]{1,0:T(8,128)(2,1)S(1)}, u32[]{:S(2)}, u32[]{:S(2)}) %collective-permute-start.33) | collective-permute-done | bytes 65568 | tf_op jit(solution)/shard_map/ppermute | solution.py:36
  335.3 2.2 fusion.139
  337.5 2.4 fusion.155
  339.9 140.1 %psum.7 = f32[1,2048]{1,0:T(1,128)} all-reduce(f32[1,2048]{1,0:T(1,128)S(1)} %bitcast.312), channel_id=1, replica_groups=mesh['section'=2,'zl'=2,'core'=2,'y'=4,'x'=4] {'zl','core','y','x'}, use_global_device_ids=true, to_apply=%region_28.29 | all-reduce | flops 2048 | bytes 16384 | tf_op jit(solution)/shard_map/psum | solution.py:274
  481.6 12.7 %collective-permute-start.26 = (bf16[128,768]{0,1:T(8,128)(2,1)S(1)}, bf16[128,768]{0,1:T(8,128)(2,1)S(1)}, u32[]{:S(2)}, u32[]{:S(2)}) collective-permute-start(bf16[128,768]{0,1:T(8,128)(2,1)S(1)} %reduce_sum.153), channel_id=1, source_target_pairs={{0,16},{16,0},{1,17},{17,1},{2,18},{18,2},{3,19},{19,3},{4,20},{20... | collective-permute-start | bytes 589832 | tf_op jit(solution)/shard_map/ppermute | solution.py:32
  494.3 3.0 collective-permute-start.28
  499.8 1.6 copy.209
  (195 shorter events, 50.5 us)
Async XLA Ops:
  7.2 18.7 %copy-start = (bf16[1,64,2048]{2,1,0:T(8,128)(2,1)S(1)}, bf16[1,64,2048]{2,1,0:T(8,128)(2,1)}, u32[]{:S(2)}) copy-start(bf16[1,64,2048]{2,1,0:T(8,128)(2,1)} %param.17) | copy-start | bytes 786436
  7.2 2.4 copy-start.3
  7.2 58.3 %all-gather.4.cloned.1.call-start = ((), (), s32[]{:S(2)}) async-start(), calls=%async_computation.2 | async-start | bytes 3342336 | tf_op jit(solution)/shard_map/all_gather | solution.py:166
  9.6 99.6 %all-gather.6.cloned.1.call-start = ((), (), s32[]{:S(2)}) async-start(), calls=%async_computation.3 | async-start | bytes 1114112 | tf_op jit(solution)/shard_map/all_gather | solution.py:169
  9.6 14.2 %collective-permute-start.1 = (bf16[128,2048]{1,0:T(8,128)(2,1)S(1)}, bf16[128,2048]{1,0:T(8,128)(2,1)S(1)}, u32[]{:S(2)}, u32[]{:S(2)}) collective-permute-start(bf16[128,2048]{1,0:T(8,128)(2,1)S(1)} %bitcast.244), channel_id=1, source_target_pairs={{0,32},{32,0},{1,33},{33,1},{2,34},{34,2},{3,35},{35,3},{4,36},{36... | collective-permute-start | bytes 1572872 | tf_op jit(solution)/shard_map/ppermute | solution.py:36
  12.2 23.0 %collective-permute-start.11 = (bf16[128,2048]{1,0:T(8,128)(2,1)}, bf16[128,2048]{1,0:T(8,128)(2,1)}, u32[]{:S(2)}, u32[]{:S(2)}) collective-permute-start(bf16[128,2048]{1,0:T(8,128)(2,1)} %bitcast.72), channel_id=1, source_target_pairs={{0,32},{32,0},{1,33},{33,1},{2,34},{34,2},{3,35},{35,3},{4,36},{36... | collective-permute-start | bytes 1572872 | tf_op jit(solution)/shard_map/ppermute | solution.py:36
  12.3 24.1 %collective-permute-start = (bf16[128,2048]{1,0:T(8,128)(2,1)S(1)}, bf16[128,2048]{1,0:T(8,128)(2,1)S(1)}, u32[]{:S(2)}, u32[]{:S(2)}) collective-permute-start(bf16[128,2048]{1,0:T(8,128)(2,1)S(1)} %bitcast.245), channel_id=1, source_target_pairs={{0,16},{16,0},{1,17},{17,1},{2,18},{18,2},{3,19},{19,3},{4,20},{20... | collective-permute-start | bytes 1572872 | tf_op jit(solution)/shard_map/ppermute | solution.py:32
  23.8 13.4 %collective-permute-start.2 = (bf16[128,2048]{1,0:T(8,128)(2,1)S(1)}, bf16[128,2048]{1,0:T(8,128)(2,1)}, u32[]{:S(2)}, u32[]{:S(2)}) collective-permute-start(bf16[128,2048]{1,0:T(8,128)(2,1)S(1)} %collective-permute-done.1), channel_id=1, source_target_pairs={{0,16},{16,0},{1,17},{17,1},{2,18},{18,2},{3,19},{19,3},{4,20},{20... | collective-permute-start | bytes 1572872 | tf_op jit(solution)/shard_map/ppermute | solution.py:32
  25.9 53.1 %collective-permute-start.10 = (bf16[128,2048]{1,0:T(8,128)(2,1)}, bf16[128,2048]{1,0:T(8,128)(2,1)}, u32[]{:S(2)}, u32[]{:S(2)}) collective-permute-start(bf16[128,2048]{1,0:T(8,128)(2,1)} %bitcast.72), channel_id=1, source_target_pairs={{0,16},{16,0},{1,17},{17,1},{2,18},{18,2},{3,19},{19,3},{4,20},{20... | collective-permute-start | bytes 1572872 | tf_op jit(solution)/shard_map/ppermute | solution.py:32
  26.6 12.3 %copy-start.45 = (f32[1,2048]{1,0:T(1,128)S(1)}, f32[1,2048]{1,0:T(1,128)}, u32[]{:S(2)}) copy-start(f32[1,2048]{1,0:T(1,128)} %param.18) | copy-start | bytes 24580
  35.1 43.9 %collective-permute-start.12 = (bf16[128,2048]{1,0:T(8,128)(2,1)}, bf16[128,2048]{1,0:T(8,128)(2,1)}, u32[]{:S(2)}, u32[]{:S(2)}) collective-permute-start(bf16[128,2048]{1,0:T(8,128)(2,1)} %collective-permute-done.11), channel_id=1, source_target_pairs={{0,16},{16,0},{1,17},{17,1},{2,18},{18,2},{3,19},{19,3},{4,20},{20... | collective-permute-start | bytes 1572872 | tf_op jit(solution)/shard_map/ppermute | solution.py:32
  38.8 2.0 copy-start.54
  77.8 36.7 %collective-permute-start.4 = (bf16[256,256]{1,0:T(8,128)(2,1)}, bf16[256,256]{1,0:T(8,128)(2,1)}, u32[]{:S(2)}, u32[]{:S(2)}) collective-permute-start(bf16[256,256]{1,0:T(8,128)(2,1)} %copy.194), channel_id=1, source_target_pairs={{0,32},{32,0},{1,33},{33,1},{2,34},{34,2},{3,35},{35,3},{4,36},{36... | collective-permute-start | bytes 393224 | tf_op jit(solution)/shard_map/ppermute | solution.py:36
  83.2 31.2 %copy-start.47 = (bf16[256,256]{1,0:T(8,128)(2,1)S(1)}, bf16[256,256]{1,0:T(8,128)(2,1)}, u32[]{:S(2)}) copy-start(bf16[256,256]{1,0:T(8,128)(2,1)} %copy.194) | copy-start | bytes 393220
  110.4 12.0 %collective-permute-start.13 = (bf16[256,512]{1,0:T(8,128)(2,1)S(1)}, bf16[256,512]{1,0:T(8,128)(2,1)S(1)}, u32[]{:S(2)}, u32[]{:S(2)}) collective-permute-start(bf16[256,512]{1,0:T(8,128)(2,1)S(1)} %get-tuple-element.381), channel_id=1, source_target_pairs={{0,16},{16,0},{1,17},{17,1},{2,18},{18,2},{3,19},{19,3},{4,20},{20... | collective-permute-start | bytes 786440 | tf_op jit(solution)/shard_map/ppermute | solution.py:32
  112.6 9.8 %collective-permute-start.14 = (bf16[256,512]{1,0:T(8,128)(2,1)S(1)}, bf16[256,512]{1,0:T(8,128)(2,1)S(1)}, u32[]{:S(2)}, u32[]{:S(2)}) collective-permute-start(bf16[256,512]{1,0:T(8,128)(2,1)S(1)} %get-tuple-element.380), channel_id=1, source_target_pairs={{0,32},{32,0},{1,33},{33,1},{2,34},{34,2},{3,35},{35,3},{4,36},{36... | collective-permute-start | bytes 786440 | tf_op jit(solution)/shard_map/ppermute | solution.py:36
  113.9 12.8 %collective-permute-start.15 = (bf16[256,512]{1,0:T(8,128)(2,1)S(1)}, bf16[256,512]{1,0:T(8,128)(2,1)S(1)}, u32[]{:S(2)}, u32[]{:S(2)}) collective-permute-start(bf16[256,512]{1,0:T(8,128)(2,1)S(1)} %get-tuple-element.379), channel_id=1, source_target_pairs={{0,48},{16,32},{32,16},{48,0},{1,49},{17,33},{33,17},{49,1},{2,50}... | collective-permute-start | bytes 786440 | tf_op jit(solution)/shard_map/ppermute | solution.py:46
  114.3 1.4 collective-permute-start.3
  114.5 1.6 collective-permute-start.5
  116.1 1.5 copy-start.48
  116.1 1.5 copy-start.49
  116.1 1.5 copy-start.50
  116.1 1.5 copy-start.51
  117.6 13.2 %collective-permute-start.6 = (bf16[256,512]{1,0:T(8,128)(2,1)S(1)}, bf16[256,512]{1,0:T(8,128)(2,1)S(1)}, u32[]{:S(2)}, u32[]{:S(2)}) collective-permute-start(bf16[256,512]{1,0:T(8,128)(2,1)S(1)} %fusion.131), channel_id=1, source_target_pairs={{0,64},{1,65},{2,66},{3,67},{4,68},{5,69},{6,70},{7,71},{8,72},{9,... | collective-permute-start | bytes 786440 | tf_op jit(solution)/shard_map/ppermute | solution.py:201
  126.7 4.2 copy-start.18
  126.9 5.5 %copy-start.34 = (bf16[256,512]{1,0:T(8,128)(2,1)}, bf16[256,512]{1,0:T(8,128)(2,1)S(1)}, u32[]{:S(2)}) copy-start(bf16[256,512]{1,0:T(8,128)(2,1)S(1)} %get-tuple-element.370) | copy-start | bytes 786436
  126.9 5.5 %copy-start.35 = (bf16[256,512]{1,0:T(8,128)(2,1)}, bf16[256,512]{1,0:T(8,128)(2,1)S(1)}, u32[]{:S(2)}) copy-start(bf16[256,512]{1,0:T(8,128)(2,1)S(1)} %get-tuple-element.371) | copy-start | bytes 786436
  127.0 5.4 %copy-start.36 = (bf16[256,512]{1,0:T(8,128)(2,1)}, bf16[256,512]{1,0:T(8,128)(2,1)S(1)}, u32[]{:S(2)}) copy-start(bf16[256,512]{1,0:T(8,128)(2,1)S(1)} %get-tuple-element.372) | copy-start | bytes 786436
  127.0 5.4 %copy-start.37 = (bf16[256,512]{1,0:T(8,128)(2,1)}, bf16[256,512]{1,0:T(8,128)(2,1)S(1)}, u32[]{:S(2)}) copy-start(bf16[256,512]{1,0:T(8,128)(2,1)S(1)} %get-tuple-element.373) | copy-start | bytes 786436
  130.8 6.9 %collective-permute-start.8 = (bf16[256,512]{1,0:T(8,128)(2,1)S(1)}, bf16[256,512]{1,0:T(8,128)(2,1)S(1)}, u32[]{:S(2)}, u32[]{:S(2)}) collective-permute-start(bf16[256,512]{1,0:T(8,128)(2,1)S(1)} %collective-permute-done.6), channel_id=1, source_target_pairs={{0,32},{32,0},{1,33},{33,1},{2,34},{34,2},{3,35},{35,3},{4,36},{36... | collective-permute-start | bytes 786440 | tf_op jit(solution)/shard_map/ppermute | solution.py:36
  132.4 7.1 %collective-permute-start.7 = (bf16[256,512]{1,0:T(8,128)(2,1)S(1)}, bf16[256,512]{1,0:T(8,128)(2,1)S(1)}, u32[]{:S(2)}, u32[]{:S(2)}) collective-permute-start(bf16[256,512]{1,0:T(8,128)(2,1)S(1)} %collective-permute-done.6), channel_id=1, source_target_pairs={{0,16},{16,0},{1,17},{17,1},{2,18},{18,2},{3,19},{19,3},{4,20},{20... | collective-permute-start | bytes 786440 | tf_op jit(solution)/shard_map/ppermute | solution.py:32
  137.7 2.9 collective-permute-start.9
  146.5 1.2 copy-start.46
  146.5 11.1 %copy-start.57 = (f32[64,1]{0,1:T(1,128)}, f32[64,1]{0,1:T(1,128)S(1)}, u32[]{:S(2)}) copy-start(f32[64,1]{0,1:T(1,128)S(1)} %get-tuple-element.153) | copy-start | bytes 772
  147.7 2.6 collective-permute-start.17
  149.7 8.0 %collective-permute-start.30 = (bf16[512,256]{1,0:T(8,128)(2,1)}, bf16[512,256]{1,0:T(8,128)(2,1)S(1)}, u32[]{:S(2)}, u32[]{:S(2)}) collective-permute-start(bf16[512,256]{1,0:T(8,128)(2,1)} %copy-done.46), channel_id=1, source_target_pairs={{0,32},{32,0},{1,33},{33,1},{2,34},{34,2},{3,35},{35,3},{4,36},{36... | collective-permute-start | bytes 786440 | tf_op jit(solution)/shard_map/ppermute | solution.py:36
  149.8 9.4 %collective-permute-start.29 = (bf16[512,256]{1,0:T(8,128)(2,1)}, bf16[512,256]{1,0:T(8,128)(2,1)S(1)}, u32[]{:S(2)}, u32[]{:S(2)}) collective-permute-start(bf16[512,256]{1,0:T(8,128)(2,1)} %copy-done.46), channel_id=1, source_target_pairs={{0,16},{16,0},{1,17},{17,1},{2,18},{18,2},{3,19},{19,3},{4,20},{20... | collective-permute-start | bytes 786440 | tf_op jit(solution)/shard_map/ppermute | solution.py:32
  150.3 9.0 %collective-permute-start.16 = (bf16[64,2048]{1,0:T(8,128)(2,1)S(1)}, bf16[64,2048]{1,0:T(8,128)(2,1)S(1)}, u32[]{:S(2)}, u32[]{:S(2)}) collective-permute-start(bf16[64,2048]{1,0:T(8,128)(2,1)S(1)} %get-tuple-element.368), channel_id=1, source_target_pairs={{0,16},{16,0},{1,17},{17,1},{2,18},{18,2},{3,19},{19,3},{4,20},{20... | collective-permute-start | bytes 786440 | tf_op jit(solution)/shard_map/ppermute | solution.py:32
  151.4 11.9 %collective-permute-start.18 = (bf16[64,2048]{1,0:T(8,128)(2,1)S(1)}, bf16[64,2048]{1,0:T(8,128)(2,1)S(1)}, u32[]{:S(2)}, u32[]{:S(2)}) collective-permute-start(bf16[64,2048]{1,0:T(8,128)(2,1)S(1)} %add_convert_fusion.3), channel_id=1, source_target_pairs={{0,32},{32,0},{1,33},{33,1},{2,34},{34,2},{3,35},{35,3},{4,36},{36... | collective-permute-start | bytes 786440 | tf_op jit(solution)/shard_map/ppermute | solution.py:36
  157.7 6.9 %copy-start.58 = (f32[64,1]{0,1:T(1,128)S(1)}, f32[64,1]{0,1:T(1,128)}, u32[]{:S(2)}) copy-start(f32[64,1]{0,1:T(1,128)} %copy-done.57) | copy-start | bytes 772
  157.7 8.4 %collective-permute-start.31 = (bf16[512,256]{1,0:T(8,128)(2,1)S(1)}, bf16[512,256]{1,0:T(8,128)(2,1)S(1)}, u32[]{:S(2)}, u32[]{:S(2)}) collective-permute-start(bf16[512,256]{1,0:T(8,128)(2,1)S(1)} %collective-permute-done.30), channel_id=1, source_target_pairs={{0,16},{16,0},{1,17},{17,1},{2,18},{18,2},{3,19},{19,3},{4,20},{20... | collective-permute-start | bytes 786440 | tf_op jit(solution)/shard_map/ppermute | solution.py:32
  164.8 80.0 %collective-permute-start.19 = (bf16[64,2048]{1,0:T(8,128)(2,1)S(1)}, bf16[64,2048]{1,0:T(8,128)(2,1)S(1)}, u32[]{:S(2)}, u32[]{:S(2)}) collective-permute-start(bf16[64,2048]{1,0:T(8,128)(2,1)S(1)} %fusion.149), channel_id=1, source_target_pairs={{64,0},{65,1},{66,2},{67,3},{68,4},{69,5},{70,6},{71,7},{72,8},{73... | collective-permute-start | bytes 786440 | tf_op jit(solution)/shard_map/ppermute | solution.py:228
  244.8 11.5 %copy-start.41 = (bf16[64,2048]{1,0:T(8,128)(2,1)}, bf16[64,2048]{1,0:T(8,128)(2,1)S(1)}, u32[]{:S(2)}) copy-start(bf16[64,2048]{1,0:T(8,128)(2,1)S(1)} %collective-permute-done.19) | copy-start | bytes 786436
  244.8 10.3 %collective-permute-start.20 = (bf16[64,2048]{1,0:T(8,128)(2,1)S(1)}, bf16[64,2048]{1,0:T(8,128)(2,1)S(1)}, u32[]{:S(2)}, u32[]{:S(2)}) collective-permute-start(bf16[64,2048]{1,0:T(8,128)(2,1)S(1)} %collective-permute-done.19), channel_id=1, source_target_pairs={{0,16},{16,0},{1,17},{17,1},{2,18},{18,2},{3,19},{19,3},{4,20},{20... | collective-permute-start | bytes 786440 | tf_op jit(solution)/shard_map/ppermute | solution.py:32
  246.3 7.9 %collective-permute-start.21 = (bf16[64,2048]{1,0:T(8,128)(2,1)S(1)}, bf16[64,2048]{1,0:T(8,128)(2,1)S(1)}, u32[]{:S(2)}, u32[]{:S(2)}) collective-permute-start(bf16[64,2048]{1,0:T(8,128)(2,1)S(1)} %collective-permute-done.19), channel_id=1, source_target_pairs={{0,32},{32,0},{1,33},{33,1},{2,34},{34,2},{3,35},{35,3},{4,36},{36... | collective-permute-start | bytes 786440 | tf_op jit(solution)/shard_map/ppermute | solution.py:36
  254.3 1.9 collective-permute-start.22
  256.2 1.0 copy-start.19
  260.9 1.0 copy-start.33
  261.9 7.1 %copy-start.2 = (bf16[512,2048]{1,0:T(8,128)(2,1)S(1)}, bf16[512,2048]{1,0:T(8,128)(2,1)}, u32[]{:S(2)}) copy-start(bf16[512,2048]{1,0:T(8,128)(2,1)} %fusion.129) | copy-start | bytes 6291460
  261.9 43.1 %all-to-all-start.1 = ((bf16[16,64,512]{2,1,0:T(8,128)(2,1)}), bf16[16,64,512]{2,1,0:T(8,128)(2,1)}, u32[]{:S(2)}, u32[]{:S(2)}) async-start(bf16[16,64,512]{2,1,0:T(8,128)(2,1)} %bitcast.267), calls=%async_computation.1 | async-start | bytes 2097152 | tf_op jit(solution)/shard_map/all_to_all | solution.py:62
  275.1 8.5 %copy-start.9 = (bf16[256,512]{1,0:T(8,128)(2,1)S(1)}, bf16[256,512]{1,0:T(8,128)(2,1)}, u32[]{:S(2)}) copy-start(bf16[256,512]{1,0:T(8,128)(2,1)} %copy-done.8) | copy-start | bytes 786436 | tf_op jit(solution)/shard_map/cond
  305.0 175.0 %all-to-all-start = ((bf16[16,128,768]{1,2,0:T(8,128)(2,1)}), bf16[16,128,768]{1,2,0:T(8,128)(2,1)S(1)}, u32[]{:S(2)}, u32[]{:S(2)}) async-start(bf16[16,128,768]{1,2,0:T(8,128)(2,1)} %copy.199), calls=%async_computation | async-start | bytes 6291456 | tf_op jit(solution)/shard_map/all_to_all | solution.py:62
  313.7 3.5 collective-permute-start.24
  314.9 20.4 %collective-permute-start.23 = (bf16[128,2048]{1,0:T(8,128)(2,1)}, bf16[128,2048]{1,0:T(8,128)(2,1)}, u32[]{:S(2)}, u32[]{:S(2)}) collective-permute-start(bf16[128,2048]{1,0:T(8,128)(2,1)} %get-tuple-element.366), channel_id=1, source_target_pairs={{0,16},{16,0},{1,17},{17,1},{2,18},{18,2},{3,19},{19,3},{4,20},{20... | collective-permute-start | bytes 1572872 | tf_op jit(solution)/shard_map/ppermute | solution.py:32
  319.1 18.4 %copy-start.42 = (bf16[64,2048]{1,0:T(8,128)(2,1)S(1)}, bf16[64,2048]{1,0:T(8,128)(2,1)}, u32[]{:S(2)}) copy-start(bf16[64,2048]{1,0:T(8,128)(2,1)} %copy-done.41) | copy-start | bytes 786436
  319.1 16.2 %collective-permute-start.25 = (bf16[128,2048]{1,0:T(8,128)(2,1)}, bf16[128,2048]{1,0:T(8,128)(2,1)}, u32[]{:S(2)}, u32[]{:S(2)}) collective-permute-start(bf16[128,2048]{1,0:T(8,128)(2,1)} %add_convert_fusion.1), channel_id=1, source_target_pairs={{0,32},{32,0},{1,33},{33,1},{2,34},{34,2},{3,35},{35,3},{4,36},{36... | collective-permute-start | bytes 1572872 | tf_op jit(solution)/shard_map/ppermute | solution.py:36
  321.0 16.5 %copy-start.4 = (bf16[1,1,128,2048]{3,2,1,0:T(8,128)(2,1)S(1)}, bf16[1,1,128,2048]{3,2,1,0:T(8,128)(2,1)}, u32[]{:S(2)}) copy-start(bf16[1,1,128,2048]{3,2,1,0:T(8,128)(2,1)} %param.15) | copy-start | bytes 1572868
  321.0 13.3 %collective-permute-start.33 = (bf16[64,512]{1,0:T(8,128)(2,1)S(1)}, bf16[64,512]{1,0:T(8,128)(2,1)S(1)}, u32[]{:S(2)}, u32[]{:S(2)}) collective-permute-start(bf16[64,512]{1,0:T(8,128)(2,1)S(1)} %reduce_sum.154), channel_id=1, source_target_pairs={{0,32},{32,0},{1,33},{33,1},{2,34},{34,2},{3,35},{35,3},{4,36},{36... | collective-permute-start | bytes 196616 | tf_op jit(solution)/shard_map/ppermute | solution.py:36
  323.7 156.9 %collective-permute-start.32 = (bf16[64,512]{1,0:T(8,128)(2,1)S(1)}, bf16[64,512]{1,0:T(8,128)(2,1)}, u32[]{:S(2)}, u32[]{:S(2)}) collective-permute-start(bf16[64,512]{1,0:T(8,128)(2,1)S(1)} %reduce_sum.154), channel_id=1, source_target_pairs={{0,16},{16,0},{1,17},{17,1},{2,18},{18,2},{3,19},{19,3},{4,20},{20... | collective-permute-start | bytes 196616 | tf_op jit(solution)/shard_map/ppermute | solution.py:32
  334.2 146.4 %collective-permute-start.34 = (bf16[64,512]{1,0:T(8,128)(2,1)S(1)}, bf16[64,512]{1,0:T(8,128)(2,1)}, u32[]{:S(2)}, u32[]{:S(2)}) collective-permute-start(bf16[64,512]{1,0:T(8,128)(2,1)S(1)} %collective-permute-done.33), channel_id=1, source_target_pairs={{0,16},{16,0},{1,17},{17,1},{2,18},{18,2},{3,19},{19,3},{4,20},{20... | collective-permute-start | bytes 196616 | tf_op jit(solution)/shard_map/ppermute | solution.py:32
  480.5 13.8 %collective-permute-start.27 = (bf16[128,768]{0,1:T(8,128)(2,1)S(1)}, bf16[128,768]{0,1:T(8,128)(2,1)S(1)}, u32[]{:S(2)}, u32[]{:S(2)}) collective-permute-start(bf16[128,768]{0,1:T(8,128)(2,1)S(1)} %reduce_sum.153), channel_id=1, source_target_pairs={{0,32},{32,0},{1,33},{33,1},{2,34},{34,2},{3,35},{35,3},{4,36},{36... | collective-permute-start | bytes 589832 | tf_op jit(solution)/shard_map/ppermute | solution.py:36
  481.6 16.5 %collective-permute-start.26 = (bf16[128,768]{0,1:T(8,128)(2,1)S(1)}, bf16[128,768]{0,1:T(8,128)(2,1)S(1)}, u32[]{:S(2)}, u32[]{:S(2)}) collective-permute-start(bf16[128,768]{0,1:T(8,128)(2,1)S(1)} %reduce_sum.153), channel_id=1, source_target_pairs={{0,16},{16,0},{1,17},{17,1},{2,18},{18,2},{3,19},{19,3},{4,20},{20... | collective-permute-start | bytes 589832 | tf_op jit(solution)/shard_map/ppermute | solution.py:32
  494.3 4.1 collective-permute-start.28
  499.3 2.1 copy-start.1
  (5 other events, 4.0 us)
Sparse Core Ops, SparseCore 0:
  10.7 54.7 all-gather.3
  67.7 41.4 all-gather.5
